TPU v7x, 128 devices: a whole 4x4x4 slice. The times are simulated.
128 devices in a mesh: rep: 8 (over x_lo, z), shard: 16 (over y, x_hi, core).
Axes of the slice: x: 4 (x_hi: 2, x_lo: 2; x = x_hi * 2 + x_lo), y: 4, z: 4, core: 2. Of those that a mesh axis runs over, the one named last changes fastest.
Arguments:
- hidden_in: bfloat16 [32768, 2048], P(('rep', 'shard')), may hold values from -6 to 6
- cotangent: bfloat16 [32768, 2048], P(('rep', 'shard')), may hold values from -6 to 6
- segment_ids: int32 [32768], P('rep'), may hold values from 0 to 2, as said below
- positions: int32 [32768], P('rep'), may hold values from 0 to 3583, as said below
- attn_gain: float32 [2048], P('shard'), may hold values from 0.25 to 1.75
- query_gain: float32 [128], replicated, may hold values from 0.25 to 1.75
- key_gain: float32 [128], replicated, may hold values from 0.25 to 1.75
- query_weight: float32 [2048, 2048], P('shard'), may hold values from -0.125 to 0.125
- key_weight: float32 [2048, 1024], P('shard'), may hold values from -0.125 to 0.125
- value_weight: float32 [2048, 1024], P('shard'), may hold values from -0.125 to 0.125
- out_weight: float32 [2048, 2048], P('shard'), may hold values from -3 to 3
- mlp_gain: float32 [2048], P('shard'), may hold values from 0.25 to 1.75
- gate_weight: float32 [2048, 6144], P('shard'), may hold values from -0.125 to 0.125
- up_weight: float32 [2048, 6144], P('shard'), may hold values from -0.125 to 0.125
- down_weight: float32 [2048, 6144], P('shard'), may hold values from -0.078125 to 0.078125
Outputs:
- output: bfloat16 [32768, 2048], P(('rep', 'shard'))
- hidden_grad: bfloat16 [32768, 2048], P(('rep', 'shard'))
- attn_gain_grad: float32 [2048], P('shard')
- query_gain_grad: float32 [128], replicated
- key_gain_grad: float32 [128], replicated
- query_weight_grad: float32 [2048, 2048], P('shard')
- key_weight_grad: float32 [2048, 1024], P('shard')
- value_weight_grad: float32 [2048, 1024], P('shard')
- out_weight_grad: float32 [2048, 2048], P('shard')
- mlp_gain_grad: float32 [2048], P('shard')
- gate_weight_grad: float32 [2048, 6144], P('shard')
- up_weight_grad: float32 [2048, 6144], P('shard')
- down_weight_grad: float32 [2048, 6144], P('shard')
Inputs may be any that keep to these rules, and one draw needn't show every extreme that they name: `segment_ids`: within the 4096 rows of each index of rep, one prompt of 3072 rows (segment 0) and 2 continuations of 512 rows (segments 1 to 2) are laid out; each index of shard holds 256 consecutive rows of the order prompt, continuation 1, ..., and these runs are placed on the devices in a drawn order. Prompt rows have positions 0 to 3071 in order; continuation rows have positions 3072 to 3583 in order, in the layout of segment_ids.
All inputs are finite; a program needn't handle non-finite values.
Results may differ from a plain program's by a relative error of at most 0.025.
Values may be sent and summed in bfloat16 or wider, within the bound.
No kernel may reach another device: no remote copies, remote signals or barrier semaphores. Data moves between devices by JAX's collectives and lax.ppermute only.
A program may use at most 384 MiB of HBM per device.

v0:
```python
import jax
import jax.numpy as jnp
from jax import lax
from jax.sharding import PartitionSpec as P

HEADS = 16
KV_HEADS = 8
HEAD_DIM = 128
Q_DIM = 2048
KV_DIM = 1024
norm_eps = 1e-06
rope_base = 1000000.0
masked_score = -1e30
contract_first = (((0,), (0,)), ((), ()))
contract_last = (((1,), (1,)), ((), ()))


def normalize(values):
    return values * lax.rsqrt(jnp.mean(values * values, axis=-1, keepdims=True) + norm_eps)


def scaled_norm(values, scale):
    return normalize(values) * scale


def rotate(values, places):
    half_dim = values.shape[-1] // 2
    frequency = rope_base ** (-2.0 * jnp.arange(half_dim, dtype=jnp.float32) / values.shape[-1])
    angles = places.astype(jnp.float32)[:, None] * frequency[None, :]
    cosine = jnp.cos(angles)[:, None, :]
    sine_part = jnp.sin(angles)[:, None, :]
    first_half = values[..., :half_dim]
    second_half = values[..., half_dim:]
    return jnp.concatenate(
        [
            first_half * cosine - second_half * sine_part,
            second_half * cosine + first_half * sine_part,
        ],
        axis=-1,
    )


def swiglu(gate_in, upper_in):
    return jax.nn.silu(gate_in) * upper_in


def owner_share(left, right):
    term = lax.dot_general(left, right, contract_first, preferred_element_type=jnp.float32)
    return lax.psum_scatter(
        term.astype(jnp.bfloat16), "shard", scatter_dimension=0, tiled=True
    ).astype(jnp.float32)


def local(
    hidden_in,
    cotangent,
    segment_ids,
    positions,
    attn_gain,
    query_gain,
    key_gain,
    query_weight,
    key_weight,
    value_weight,
    out_weight,
    mlp_gain,
    gate_weight,
    up_weight,
    down_weight,
):
    row_count = hidden_in.shape[0]
    own_rows = attn_gain.shape[0]
    my_index = lax.axis_index("shard")
    group_rows = segment_ids.shape[0]
    group_size = HEADS // KV_HEADS
    score_scale = HEAD_DIM ** (-0.5)
    own_segments = lax.dynamic_slice_in_dim(segment_ids, my_index * row_count, row_count)
    own_places = lax.dynamic_slice_in_dim(positions, my_index * row_count, row_count)
    hidden = hidden_in.astype(jnp.float32)
    gain_low, query_low, key_low, value_low, out_low = (
        lax.all_gather(attn_gain.astype(jnp.bfloat16), "shard", axis=0, tiled=True),
        lax.all_gather(query_weight.astype(jnp.bfloat16), "shard", axis=0, tiled=True),
        lax.all_gather(key_weight.astype(jnp.bfloat16), "shard", axis=0, tiled=True),
        lax.all_gather(value_weight.astype(jnp.bfloat16), "shard", axis=0, tiled=True),
        lax.all_gather(out_weight.astype(jnp.bfloat16), "shard", axis=0, tiled=True),
    )
    attn_scale = gain_low.astype(jnp.float32)
    first_in = scaled_norm(hidden, attn_scale).astype(jnp.bfloat16)
    query_pre = jnp.dot(first_in, query_low, preferred_element_type=jnp.float32)
    key_pre = jnp.dot(first_in, key_low, preferred_element_type=jnp.float32)
    value_pre = jnp.dot(first_in, value_low, preferred_element_type=jnp.float32)

    def head_prep(query_part, key_part, query_scale, key_scale):
        query_out = rotate(
            normalize(query_part.reshape(row_count, HEADS, HEAD_DIM)) * query_scale, own_places
        )
        key_out = rotate(
            normalize(key_part.reshape(row_count, KV_HEADS, HEAD_DIM)) * key_scale, own_places
        )
        return (query_out, key_out)

    (queries, key_act), prep_back = jax.vjp(head_prep, query_pre, key_pre, query_gain, key_gain)
    key_send = key_act.astype(jnp.bfloat16).reshape(row_count, KV_DIM)
    value_send = value_pre.astype(jnp.bfloat16)
    key_all, value_all = (
        lax.all_gather(key_send, "shard", axis=0, tiled=True),
        lax.all_gather(value_send, "shard", axis=0, tiled=True),
    )
    visible = (positions[None, :] <= own_places[:, None]) & (
        (segment_ids[None, :] == 0) | (segment_ids[None, :] == own_segments[:, None])
    )
    tiled_mask = jnp.tile(visible, (group_size, 1))
    query_heads = (
        queries.astype(jnp.bfloat16)
        .reshape(row_count, KV_HEADS, group_size, HEAD_DIM)
        .transpose(1, 2, 0, 3)
        .reshape(KV_HEADS, group_size * row_count, HEAD_DIM)
    )

    def head_scores(head_index):
        head_keys = lax.dynamic_slice_in_dim(key_all, head_index * HEAD_DIM, HEAD_DIM, 1)
        raw_scores = (
            lax.dot_general(
                query_heads[head_index],
                head_keys,
                contract_last,
                preferred_element_type=jnp.float32,
            )
            * score_scale
        )
        return (jnp.where(tiled_mask, raw_scores, masked_score), head_keys)

    def forward_head(head_index):
        scores, head_keys = head_scores(head_index)
        row_max = jnp.max(scores, axis=-1, keepdims=True)
        unscaled = jnp.exp(scores - row_max)
        row_total = jnp.sum(unscaled, axis=-1, keepdims=True)
        probabilities = unscaled / row_total
        head_values = lax.dynamic_slice_in_dim(value_all, head_index * HEAD_DIM, HEAD_DIM, 1)
        head_mixed = jnp.dot(
            probabilities.astype(jnp.bfloat16), head_values, preferred_element_type=jnp.float32
        )
        return (head_mixed, row_max + jnp.log(row_total))

    mixed_heads, log_totals = lax.map(forward_head, jnp.arange(KV_HEADS))
    mixed_out = (
        mixed_heads.reshape(KV_HEADS, group_size, row_count, HEAD_DIM)
        .transpose(2, 0, 1, 3)
        .reshape(row_count, Q_DIM)
    )
    mixed_low = mixed_out.astype(jnp.bfloat16)
    attn_out = lax.dot_general(
        mixed_low, out_low, contract_last, preferred_element_type=jnp.float32
    )
    middle = hidden + attn_out
    second_norm = normalize(middle)
    gate_cast = gate_weight.astype(jnp.bfloat16)
    up_cast = up_weight.astype(jnp.bfloat16)
    down_cast = down_weight.astype(jnp.bfloat16)
    gain_piece = lax.all_gather(mlp_gain.astype(jnp.bfloat16), "shard", axis=0, tiled=True)
    gate_piece = lax.all_gather(gate_cast, "shard", axis=0, tiled=True)
    up_piece = lax.all_gather(up_cast, "shard", axis=0, tiled=True)
    columns = second_norm
    piece_in = (columns * gain_piece.astype(jnp.float32)).astype(jnp.bfloat16)
    gate_act = jnp.dot(piece_in, gate_piece, preferred_element_type=jnp.float32)
    up_act = jnp.dot(piece_in, up_piece, preferred_element_type=jnp.float32)
    mlp_scale = gain_piece.astype(jnp.float32)
    activated, swiglu_back = jax.vjp(swiglu, gate_act, up_act)
    inner_low = activated.astype(jnp.bfloat16)
    mlp_out = lax.dot_general(
        inner_low,
        lax.all_gather(down_cast, "shard", axis=0, tiled=True),
        contract_last,
        preferred_element_type=jnp.float32,
    )
    output = (middle + mlp_out).astype(jnp.bfloat16)
    cot_float = cotangent.astype(jnp.float32)
    columns = cotangent
    inner_grad = jnp.dot(
        columns,
        lax.all_gather(down_cast, "shard", axis=0, tiled=True),
        preferred_element_type=jnp.float32,
    )
    gate_grad, upper_grad = swiglu_back(inner_grad)
    gate_grad_low = gate_grad.astype(jnp.bfloat16)
    upper_grad_low = upper_grad.astype(jnp.bfloat16)
    block = lax.dot_general(
        gate_grad_low,
        lax.all_gather(gate_cast, "shard", axis=0, tiled=True),
        contract_last,
        preferred_element_type=jnp.float32,
    ) + lax.dot_general(
        upper_grad_low,
        lax.all_gather(up_cast, "shard", axis=0, tiled=True),
        contract_last,
        preferred_element_type=jnp.float32,
    )
    _, second_back = jax.vjp(scaled_norm, middle, mlp_scale)
    middle_part, mlp_gain_part = second_back(block)
    middle_grad = cot_float + middle_part
    middle_low = middle_grad.astype(jnp.bfloat16)
    mixed_grad_low = jnp.dot(middle_low, out_low, preferred_element_type=jnp.float32).astype(
        jnp.bfloat16
    )
    mixed_grad_heads = (
        mixed_grad_low.reshape(row_count, KV_HEADS, group_size, HEAD_DIM)
        .transpose(1, 2, 0, 3)
        .reshape(KV_HEADS, group_size * row_count, HEAD_DIM)
    )

    def backward_head(head_index, running):
        query_grads, key_grads, value_grads = running
        scores, head_keys = head_scores(head_index)
        probabilities = jnp.exp(scores - log_totals[head_index])
        head_values = lax.dynamic_slice_in_dim(value_all, head_index * HEAD_DIM, HEAD_DIM, 1)
        head_out_grad = mixed_grad_heads[head_index]
        prob_grad = lax.dot_general(
            head_out_grad, head_values, contract_last, preferred_element_type=jnp.float32
        )
        score_grad = probabilities * (
            prob_grad - jnp.sum(probabilities * prob_grad, axis=-1, keepdims=True)
        )
        score_low = score_grad.astype(jnp.bfloat16)
        query_part = jnp.dot(score_low, head_keys, preferred_element_type=jnp.float32) * score_scale
        key_part = (
            lax.dot_general(
                score_low,
                query_heads[head_index],
                contract_first,
                preferred_element_type=jnp.float32,
            )
            * score_scale
        )
        value_part = lax.dot_general(
            probabilities.astype(jnp.bfloat16),
            head_out_grad,
            contract_first,
            preferred_element_type=jnp.float32,
        )
        return (
            lax.dynamic_update_index_in_dim(query_grads, query_part, head_index, 0),
            lax.dynamic_update_slice_in_dim(key_grads, key_part, head_index * HEAD_DIM, 1),
            lax.dynamic_update_slice_in_dim(value_grads, value_part, head_index * HEAD_DIM, 1),
        )

    start_grads = (
        jnp.zeros((KV_HEADS, group_size * row_count, HEAD_DIM), jnp.float32),
        jnp.zeros((group_rows, KV_DIM), jnp.float32),
        jnp.zeros((group_rows, KV_DIM), jnp.float32),
    )
    query_grads, key_grads, value_grads = lax.fori_loop(0, KV_HEADS, backward_head, start_grads)
    key_grad_own, value_grad_own = (
        lax.psum_scatter(
            key_grads.astype(jnp.bfloat16), "shard", scatter_dimension=0, tiled=True
        ).astype(jnp.float32),
        lax.psum_scatter(
            value_grads.astype(jnp.bfloat16), "shard", scatter_dimension=0, tiled=True
        ).astype(jnp.float32),
    )
    query_grad = (
        query_grads.reshape(KV_HEADS, group_size, row_count, HEAD_DIM)
        .transpose(2, 0, 1, 3)
        .reshape(row_count, HEADS, HEAD_DIM)
    )
    query_pre_grad, key_pre_grad, query_gain_part, key_gain_part = prep_back(
        (query_grad, key_grad_own.reshape(row_count, KV_HEADS, HEAD_DIM))
    )
    query_pre_low = query_pre_grad.astype(jnp.bfloat16)
    key_pre_low = key_pre_grad.astype(jnp.bfloat16)
    value_pre_low = value_grad_own.astype(jnp.bfloat16)
    first_grad = (
        lax.dot_general(query_pre_low, query_low, contract_last, preferred_element_type=jnp.float32)
        + lax.dot_general(key_pre_low, key_low, contract_last, preferred_element_type=jnp.float32)
        + lax.dot_general(
            value_pre_low, value_low, contract_last, preferred_element_type=jnp.float32
        )
    )
    _, first_back = jax.vjp(scaled_norm, hidden, attn_scale)
    hidden_part, attn_gain_part = first_back(first_grad)
    hidden_grad = (middle_grad + hidden_part).astype(jnp.bfloat16)
    query_share = owner_share(first_in, query_pre_low)
    key_share = owner_share(first_in, key_pre_low)
    value_share = owner_share(first_in, value_pre_low)
    out_share = owner_share(middle_low, mixed_low)
    gate_share, up_share, down_share = (
        owner_share(piece_in, gate_grad_low),
        owner_share(piece_in, upper_grad_low),
        owner_share(cotangent, inner_low),
    )
    gain_totals = lax.psum(
        (attn_gain_part, mlp_gain_part, query_gain_part, key_gain_part), ("rep", "shard")
    )
    attn_gain_out = lax.dynamic_slice_in_dim(gain_totals[0], my_index * own_rows, own_rows)
    mlp_gain_out = lax.dynamic_slice_in_dim(gain_totals[1], my_index * own_rows, own_rows)
    totals = (
        lax.psum(query_share.astype(jnp.bfloat16), "rep").astype(jnp.float32),
        lax.psum(key_share.astype(jnp.bfloat16), "rep").astype(jnp.float32),
        lax.psum(value_share.astype(jnp.bfloat16), "rep").astype(jnp.float32),
        lax.psum(out_share.astype(jnp.bfloat16), "rep").astype(jnp.float32),
        lax.psum(gate_share.astype(jnp.bfloat16), "rep").astype(jnp.float32),
        lax.psum(up_share.astype(jnp.bfloat16), "rep").astype(jnp.float32),
        lax.psum(down_share.astype(jnp.bfloat16), "rep").astype(jnp.float32),
    )
    return (
        output,
        hidden_grad,
        attn_gain_out,
        gain_totals[2],
        gain_totals[3],
        totals[0],
        totals[1],
        totals[2],
        totals[3],
        mlp_gain_out,
        totals[4],
        totals[5],
        totals[6],
    )


def solution(mesh):
    in_specs = (
        P(("rep", "shard"), None),
        P(("rep", "shard"), None),
        P("rep"),
        P("rep"),
        P("shard"),
        P(),
        P(),
        P("shard", None),
        P("shard", None),
        P("shard", None),
        P("shard", None),
        P("shard"),
        P("shard", None),
        P("shard", None),
        P("shard", None),
    )
    out_specs = (
        P(("rep", "shard"), None),
        P(("rep", "shard"), None),
        P("shard"),
        P(),
        P(),
        P("shard", None),
        P("shard", None),
        P("shard", None),
        P("shard", None),
        P("shard"),
        P("shard", None),
        P("shard", None),
        P("shard", None),
    )
    return jax.shard_map(local, mesh=mesh, in_specs=in_specs, out_specs=out_specs, check_vma=False)
```

profile of v0, /device:TPU:1, one launch (start us, length us, event | category | flops | bytes accessed | tf_op | source)
XLA Modules:
  0.0 2547.6 jit_solution(4251775933046974446)
XLA Ops:
  13.2 25.6 %all-gather = bf16[16,1,128]{2,1,0:T(2,128)(2,1)S(1)} all-gather(bf16[1,1,128]{2,1,0:T(2,128)(2,1)S(1)} %convert_bitcast_fusion.3), channel_id=1, replica_groups=mesh['rep'=8,'shard'=16] {'shard'}, dimensions={0}, use_global_device_ids=true | all-gather | bytes 4352 | tf_op jit(solution)/shard_map/all_gather | solution.py:81
  40.4 29.4 %all-gather.14.cloned.1.call-done = bf16[2048,1024]{1,0:T(8,128)(2,1)} async-done(((bf16[128,1024]{1,0:T(8,128)(2,1)}), bf16[2048,1024]{1,0:T(8,128)(2,1)}) %all-gather.14.cloned.1.call-update) | async-done | bytes 4194320 | tf_op jit(solution)/shard_map/all_gather | solution.py:83
  76.2 49.7 %all-gather.18.cloned.1.call-done = bf16[2048,1024]{1,0:T(8,128)(2,1)} async-done(((bf16[128,1024]{1,0:T(8,128)(2,1)}), bf16[2048,1024]{1,0:T(8,128)(2,1)}) %all-gather.18.cloned.1.call-update) | async-done | bytes 4194320 | tf_op jit(solution)/shard_map/all_gather | solution.py:84
  141.4 19.9 all-gather.1
  163.5 36.2 %all-gather.12.cloned.1.call-done = bf16[2048,2048]{1,0:T(8,128)(2,1)} async-done(((bf16[128,2048]{1,0:T(8,128)(2,1)}), bf16[2048,2048]{1,0:T(8,128)(2,1)}) %all-gather.12.cloned.1.call-update) | async-done | bytes 8388624 | tf_op jit(solution)/shard_map/all_gather | solution.py:82
  214.9 58.4 %all-gather.16.cloned.1.call-done = bf16[4096,1024]{1,0:T(8,128)(2,1)} async-done(((bf16[256,1024]{1,0:T(8,128)(2,1)}), bf16[4096,1024]{1,0:T(8,128)(2,1)}) %all-gather.16.cloned.1.call-update) | async-done | bytes 8388624 | tf_op jit(solution)/shard_map/all_gather | solution.py:106
  273.4 73.6 %all-gather.20.cloned.1.call-done = bf16[4096,1024]{1,0:T(8,128)(2,1)} async-done(((bf16[256,1024]{1,0:T(8,128)(2,1)}), bf16[4096,1024]{1,0:T(8,128)(2,1)}) %all-gather.20.cloned.1.call-update) | async-done | bytes 8388624 | tf_op jit(solution)/shard_map/all_gather | solution.py:107
  347.0 118.2 %while.33 = (s32[]{:T(128)}, bf16[8,512,128]{2,1,0:T(8,128)(2,1)}, f32[8,512,1]{1,2,0:T(1,128)S(1)}, s32[8]{0:T(128)S(1)}, bf16[8,512,128]{2,1,0:T(8,128)(2,1)},...) while((s32[]{:T(128)}, bf16[8,512,128]{2,1,0:T(8,128)(2,1)}, ...), condition=%wide.region_6.7_spmd.clone.clone, body=%wide.region_3.6_spmd.clone.sunk.clone | while | flops 1098907136 | bytes 39211712 | solution.py:145
  475.4 93.1 %all-gather.24.cloned.1.call-done = bf16[2048,6144]{1,0:T(8,128)(2,1)} async-done(((bf16[128,6144]{1,0:T(8,128)(2,1)}), bf16[2048,6144]{1,0:T(8,128)(2,1)}) %all-gather.24.cloned.1.call-update) | async-done | bytes 25165840 | tf_op jit(solution)/shard_map/all_gather | solution.py:161
  583.2 133.5 %all-gather.26.cloned.1.call-done = bf16[2048,6144]{1,0:T(8,128)(2,1)} async-done(((bf16[128,6144]{1,0:T(8,128)(2,1)}), bf16[2048,6144]{1,0:T(8,128)(2,1)}) %all-gather.26.cloned.1.call-update) | async-done | bytes 25165840 | tf_op jit(solution)/shard_map/all_gather | solution.py:162
  731.1 133.9 %all-gather.28.cloned.1.call-done = bf16[2048,6144]{1,0:T(8,128)(2,1)} async-done(((bf16[128,6144]{1,0:T(8,128)(2,1)}), bf16[2048,6144]{1,0:T(8,128)(2,1)}) %all-gather.28.cloned.1.call-update) | async-done | bytes 25165840 | tf_op jit(solution)/shard_map/all_gather | solution.py:172
  865.0 18.8 multiply_convert_fusion.1
  934.6 252.0 %while.34 = (s32[]{:T(128)}, f32[8,512,128]{2,1,0:T(8,128)}, bf16[4096,1024]{1,0:T(8,128)(2,1)}, bf16[4096,1024]{1,0:T(8,128)(2,1)}, bf16[8,512,128]{2,1,0:T(8,1...) while((s32[]{:T(128)}, f32[8,512,128]{2,1,0:T(8,128)}, ...), condition=%wide.region_11.12_spmd.clone.clone, body=%wide.region_9.11_spmd.clone.sunk.clone | while | flops 2703818240 | bytes 105657016 | solution.py:251
  1204.5 32.8 %copy.74 = bf16[2048,6144]{1,0:T(8,128)(2,1)} copy(bf16[2048,6144]{0,1:T(8,128)(2,1)} %convert_bitcast_fusion) | data formatting | bytes 50331648
  1295.7 95.0 %reduce-scatter.14.cloned.1.call-done = bf16[256,1024]{1,0:T(8,128)(2,1)} async-done(((bf16[4096,1024]{1,0:T(8,128)(2,1)}), bf16[256,1024]{1,0:T(8,128)(2,1)}) %reduce-scatter.14.cloned.1.call-update) | async-done | bytes 524304 | tf_op jit(solution)/shard_map/reduce_scatter | solution.py:256
  1396.3 19.2 convolution_convert_fusion.1
  1433.9 150.6 %reduce-scatter.28.cloned.1.call-done = bf16[128,6144]{1,0:T(8,128)(2,1)} async-done(((bf16[2048,6144]{1,0:T(8,128)(2,1)}), bf16[128,6144]{1,0:T(8,128)(2,1)}) %reduce-scatter.28.cloned.1.call-update) | async-done | bytes 1572880
  1587.1 101.4 %reduce-scatter.16.cloned.1.call-done = bf16[128,2048]{1,0:T(8,128)(2,1)} async-done(((bf16[2048,2048]{1,0:T(8,128)(2,1)}), bf16[128,2048]{1,0:T(8,128)(2,1)}) %reduce-scatter.16.cloned.1.call-update) | async-done | bytes 524304 | tf_op jit(solution)/shard_map/reduce_scatter | solution.py:49
  1688.5 105.3 %reduce-scatter.22.cloned.1.call-done = bf16[128,2048]{1,0:T(8,128)(2,1)} async-done(((bf16[2048,2048]{1,0:T(8,128)(2,1)}), bf16[128,2048]{1,0:T(8,128)(2,1)}) %reduce-scatter.22.cloned.1.call-update) | async-done | bytes 524304 | tf_op jit(solution)/shard_map/reduce_scatter | solution.py:49
  1793.8 82.8 %reduce-scatter.18.cloned.1.call-done = bf16[128,1024]{1,0:T(8,128)(2,1)} async-done(((bf16[2048,1024]{1,0:T(8,128)(2,1)}), bf16[128,1024]{1,0:T(8,128)(2,1)}) %reduce-scatter.18.cloned.1.call-update) | async-done | bytes 262160 | tf_op jit(solution)/shard_map/reduce_scatter | solution.py:49
  1876.6 83.7 %reduce-scatter.20.cloned.1.call-done = bf16[128,1024]{1,0:T(8,128)(2,1)} async-done(((bf16[2048,1024]{1,0:T(8,128)(2,1)}), bf16[128,1024]{1,0:T(8,128)(2,1)}) %reduce-scatter.20.cloned.1.call-update) | async-done | bytes 262160 | tf_op jit(solution)/shard_map/reduce_scatter | solution.py:49
  1960.3 194.3 %reduce-scatter.24.cloned.1.call-done = bf16[128,6144]{1,0:T(8,128)(2,1)} async-done(((bf16[2048,6144]{1,0:T(8,128)(2,1)}), bf16[128,6144]{1,0:T(8,128)(2,1)}) %reduce-scatter.24.cloned.1.call-update) | async-done | bytes 1572880 | tf_op jit(solution)/shard_map/reduce_scatter | solution.py:49
  2154.6 192.4 %reduce-scatter.26.cloned.1.call-done = bf16[128,6144]{1,0:T(8,128)(2,1)} async-done(((bf16[2048,6144]{1,0:T(8,128)(2,1)}), bf16[128,6144]{1,0:T(8,128)(2,1)}) %reduce-scatter.26.cloned.1.call-update) | async-done | bytes 1572880 | tf_op jit(solution)/shard_map/reduce_scatter | solution.py:49
  2376.1 148.8 %all-reduce.4 = (f32[2048]{0:T(1024)S(1)}, f32[128]{0:T(128)}, f32[128]{0:T(128)}, f32[2048]{0:T(1024)S(1)}) all-reduce(f32[2048]{0:T(1024)S(1)} %get-tuple-element.356, f32[128]{0:T(128)S(1)} %copy-done.52, f32[128]{0:T(128)S(1)} %get-tuple-element.358, f32[2048]{0:T(1024)S(1)} %copy-done.47), channel_id=1, replica_groups=mesh['rep'=8,'shard'=16] {'rep','shard'}, use_global_device_ids=true, to_apply=%region_18.19 | all-reduce | flops 4352 | bytes 34816 | tf_op jit(solution)/shard_map/psum | solution.py:290
  (374 shorter events, 632.7 us)
Async XLA Ops:
  7.2 62.6 %all-gather.14.cloned.1.call-start = ((), (), s32[]{:S(2)}) async-start(), calls=%async_computation.10 | async-start | bytes 4456448 | tf_op jit(solution)/shard_map/all_gather | solution.py:83
  9.1 116.8 %all-gather.18.cloned.1.call-start = ((), (), s32[]{:S(2)}) async-start(), calls=%async_computation.12 | async-start | bytes 4456448 | tf_op jit(solution)/shard_map/all_gather | solution.py:84
  11.0 188.8 %all-gather.12.cloned.1.call-start = ((), (), s32[]{:S(2)}) async-start(), calls=%async_computation.9 | async-start | bytes 8912896 | tf_op jit(solution)/shard_map/all_gather | solution.py:82
  13.2 260.2 %all-gather.16.cloned.1.call-start = ((), (), s32[]{:S(2)}) async-start(), calls=%async_computation.11 | async-start | bytes 8912896 | tf_op jit(solution)/shard_map/all_gather | solution.py:106
  38.9 160.9 %copy-start.30 = (f32[16,1,128]{2,1,0:T(1,128)}, f32[16,1,128]{2,1,0:T(1,128)S(1)}, u32[]{:S(2)}) copy-start(f32[16,1,128]{2,1,0:T(1,128)S(1)} %convert_element_type.240) | copy-start | bytes 24580
  39.8 160.0 %copy-start.39 = (f32[256]{0:T(256)}, f32[256]{0:T(256)S(1)}, u32[]{:S(2)}) copy-start(f32[256]{0:T(256)S(1)} %fusion.64) | copy-start | bytes 3076
  40.3 171.6 %copy-start.19 = (f32[256,64]{1,0:T(8,128)}, f32[256,64]{1,0:T(8,128)S(1)}, u32[]{:S(2)}) copy-start(f32[256,64]{1,0:T(8,128)S(1)} %get-tuple-element.424) | copy-start | bytes 196612
  40.4 171.6 %copy-start.21 = (f32[256,64]{1,0:T(8,128)}, f32[256,64]{1,0:T(8,128)S(1)}, u32[]{:S(2)}) copy-start(f32[256,64]{1,0:T(8,128)S(1)} %get-tuple-element.425) | copy-start | bytes 196612
  76.2 270.9 %all-gather.20.cloned.1.call-start = ((), (), s32[]{:S(2)}) async-start(), calls=%async_computation.13 | async-start | bytes 8912896 | tf_op jit(solution)/shard_map/all_gather | solution.py:107
  130.2 337.3 %all-gather.22.cloned.1.call-start = ((), (), s32[]{:S(2)}) async-start(), calls=%async_computation.14 | async-start | bytes 8912896 | tf_op jit(solution)/shard_map/all_gather | solution.py:85
  131.2 437.4 %all-gather.24.cloned.1.call-start = ((), (), s32[]{:S(2)}) async-start(), calls=%async_computation.15 | async-start | bytes 26738688 | tf_op jit(solution)/shard_map/all_gather | solution.py:161
  134.5 582.3 %all-gather.26.cloned.1.call-start = ((), (), s32[]{:S(2)}) async-start(), calls=%async_computation.16 | async-start | bytes 26738688 | tf_op jit(solution)/shard_map/all_gather | solution.py:162
  137.9 727.1 %all-gather.28.cloned.1.call-start = ((), (), s32[]{:S(2)}) async-start(), calls=%async_computation.17 | async-start | bytes 26738688 | tf_op jit(solution)/shard_map/all_gather | solution.py:172
  141.2 1144.1 %reduce-scatter.12.cloned.1.call-start = ((), (), s32[]{:S(2)}) async-start(), calls=%async_computation.18 | async-start | bytes 8912896 | tf_op jit(solution)/shard_map/reduce_scatter | solution.py:253
  475.4 241.3 %copy-start.9 = (bf16[256,2048]{1,0:T(8,128)(2,1)}, bf16[256,2048]{1,0:T(8,128)(2,1)S(1)}, u32[]{:S(2)}) copy-start(bf16[256,2048]{1,0:T(8,128)(2,1)S(1)} %multiply_convert_fusion.3) | copy-start | bytes 3145732
  1186.7 204.0 %reduce-scatter.14.cloned.1.call-start = ((), (), s32[]{:S(2)}) async-start(), calls=%async_computation.19 | async-start | bytes 8912896 | tf_op jit(solution)/shard_map/reduce_scatter | solution.py:256
  1187.4 397.1 %reduce-scatter.28.cloned.1.call-start = ((), (), s32[]{:S(2)}) async-start(), calls=%async_computation.26 | async-start | bytes 26738688
  1237.3 451.2 %reduce-scatter.16.cloned.1.call-start = ((), (), s32[]{:S(2)}) async-start(), calls=%async_computation.20 | async-start | bytes 8912896 | tf_op jit(solution)/shard_map/reduce_scatter | solution.py:49
  1258.3 535.5 %reduce-scatter.22.cloned.1.call-start = ((), (), s32[]{:S(2)}) async-start(), calls=%async_computation.23 | async-start | bytes 8912896 | tf_op jit(solution)/shard_map/reduce_scatter | solution.py:49
  1266.8 609.8 %reduce-scatter.18.cloned.1.call-start = ((), (), s32[]{:S(2)}) async-start(), calls=%async_computation.21 | async-start | bytes 4456448 | tf_op jit(solution)/shard_map/reduce_scatter | solution.py:49
  1295.7 664.6 %reduce-scatter.20.cloned.1.call-start = ((), (), s32[]{:S(2)}) async-start(), calls=%async_computation.22 | async-start | bytes 4456448 | tf_op jit(solution)/shard_map/reduce_scatter | solution.py:49
  1395.1 759.4 %reduce-scatter.24.cloned.1.call-start = ((), (), s32[]{:S(2)}) async-start(), calls=%async_computation.24 | async-start | bytes 26738688 | tf_op jit(solution)/shard_map/reduce_scatter | solution.py:49
  1415.5 931.5 %reduce-scatter.26.cloned.1.call-start = ((), (), s32[]{:S(2)}) async-start(), calls=%async_computation.25 | async-start | bytes 26738688 | tf_op jit(solution)/shard_map/reduce_scatter | solution.py:49
  1433.8 1095.4 %all-reduce.8.cloned.1.call-start = ((), (), s32[]{:S(2)}) async-start(), calls=%async_computation.27 | async-start | bytes 12582912 | tf_op jit(solution)/shard_map/psum | solution.py:302
  (57 other events, 630.4 us)
Sparse Core Ops, SparseCore 0:
  11.1 58.6 all-gather.13
  72.8 53.0 all-gather.17
  128.9 70.7 all-gather.11
  202.6 70.6 all-gather.15
  276.3 70.6 all-gather.19
  349.3 70.6 all-gather.21
  423.1 145.3 all-gather.23
  571.5 145.1 all-gather.25
  719.8 145.1 all-gather.27
  1186.8 98.4 reduce-scatter.11
  1289.6 101.0 reduce-scatter.13
  1394.9 189.5 reduce-scatter.27
  1588.8 99.6 reduce-scatter.15
  1692.6 101.1 reduce-scatter.21
  1797.6 78.8 reduce-scatter.17
  1881.0 79.2 reduce-scatter.19
  1964.5 190.0 reduce-scatter.23
  2158.8 188.1 reduce-scatter.25
  2350.6 146.2 all-reduce.7
where the time goes:
time: 2560 us; the launch traced here: 2550 us
  waiting for transfers between devices  1630 us (64%)
  matrix products  445 us (17%)
  blocking collectives  194 us (8%)
  other arithmetic  162 us (6%)
  local copies, waits for them, and re-layouts  75.8 us (3%)
    reduce_scatter x6, waiting for transfers between devices, owner_share(): lax.psum_scatter(term.astype(jnp.bfloat16), 'shard', scatter_dimension=0,...  760 us
    unnamed x20, waiting for transfers between devices  152 us
    psum x1, blocking collectives, local(): lax.psum((attn_gain_part, mlp_gain_part, query_gain_part, key_gain_part),...  149 us
    all_gather x1, waiting for transfers between devices, local(): lax.all_gather(down_cast, 'shard', axis=0, tiled=True)  134 us
    all_gather x1, waiting for transfers between devices, local(): up_piece = lax.all_gather(up_cast, 'shard', axis=0, tiled=True)  134 us
    dot_general x16, matrix products, head_scores(): lax.dot_general(query_heads[head_index], head_keys, contract_last, prefer...  96.5 us
    reduce_scatter x1, waiting for transfers between devices, local(): lax.psum_scatter(value_grads.astype(jnp.bfloat16), 'shard', scatter_dimen...  95 us
    all_gather x1, waiting for transfers between devices, local(): gate_piece = lax.all_gather(gate_cast, 'shard', axis=0, tiled=True)  93.1 us
  transfers between devices with their start and end apart: 19, of which 17 were waited for; matrix products, arithmetic and copies ran while one was open for 13% of the time, Pallas kernels for 0%

commit v1 on v0

--- a/solution.py
+++ b/solution.py
@@ -158,7 +158,10 @@
     up_cast = up_weight.astype(jnp.bfloat16)
     down_cast = down_weight.astype(jnp.bfloat16)
     gain_piece = lax.all_gather(mlp_gain.astype(jnp.bfloat16), "shard", axis=0, tiled=True)
-    gate_piece = lax.all_gather(gate_cast, "shard", axis=0, tiled=True)
+    gate_piece = jnp.concatenate(
+        lax.all_to_all(jnp.stack([gate_cast for _ in range(lax.psum(1, "shard"))]), "shard", 0, 0),
+        0,
+    )
     up_piece = lax.all_gather(up_cast, "shard", axis=0, tiled=True)
     columns = second_norm
     piece_in = (columns * gain_piece.astype(jnp.float32)).astype(jnp.bfloat16)

time: 2560 us -> 2750 us (1.074)
  blocking collectives: 194 us -> 491 us
  waiting for transfers between devices: 1630 us -> 1530 us
    all_gather x1, blocking collectives: 19.9 us -> 317 us  [local(): lax.all_gather(mlp_gain.astype(jnp.bfloat16), 'shard', axis=0, tiled=True)]
    all_gather x1, waiting for transfers between devices: 134 us -> 77.1 us  [local(): up_piece = lax.all_gather(up_cast, 'shard', axis=0, tiled=True)]
    all_gather x1, waiting for transfers between devices: 58.4 us -> 14.6 us  [local(): lax.all_gather(key_send, 'shard', axis=0, tiled=True)]
    all_gather x1, waiting for transfers between devices: 36.2 us -> 0.02 us  [local(): lax.all_gather(query_weight.astype(jnp.bfloat16), 'shard', axis=0, tiled=...]
    all_gather x1, waiting for transfers between devices: 93.1 us -> 127 us  [local(): lax.all_gather(gate_cast, 'shard', axis=0, tiled=True)]
  transfers between devices with their start and end apart: 19 -> 20, of which waited for: 17 -> 16; matrix products, arithmetic and copies ran while one was open for 13% -> 13% of each run, Pallas kernels for 0% -> 0%
where the time goes in v1:
time: 2750 us; the launch traced here: 2730 us
  waiting for transfers between devices  1530 us (56%)
  blocking collectives  491 us (18%)
  matrix products  422 us (15%)
  other arithmetic  160 us (6%)
  local copies, waits for them, and re-layouts  85.2 us (3%)
    reduce_scatter x6, waiting for transfers between devices, owner_share(): lax.psum_scatter(term.astype(jnp.bfloat16), 'shard', scatter_dimension=0,...  760 us
    all_gather x1, blocking collectives, local(): lax.all_gather(mlp_gain.astype(jnp.bfloat16), 'shard', axis=0, tiled=True)  317 us
    unnamed x20, waiting for transfers between devices  151 us
    psum x1, blocking collectives, local(): lax.psum((attn_gain_part, mlp_gain_part, query_gain_part, key_gain_part),...  149 us
    all_gather x1, waiting for transfers between devices, local(): lax.all_gather(down_cast, 'shard', axis=0, tiled=True)  134 us
    all_gather x1, waiting for transfers between devices, local(): lax.all_gather(gate_cast, 'shard', axis=0, tiled=True)  127 us
    dot_general x16, matrix products, head_scores(): lax.dot_general(query_heads[head_index], head_keys, contract_last, prefer...  96.1 us
    reduce_scatter x1, waiting for transfers between devices, local(): lax.psum_scatter(value_grads.astype(jnp.bfloat16), 'shard', scatter_dimen...  94.9 us
  transfers between devices with their start and end apart: 20, of which 16 were waited for; matrix products, arithmetic and copies ran while one was open for 13% of the time, Pallas kernels for 0%

profile of v1, /device:TPU:1, one launch (start us, length us, event | category | flops | bytes accessed | tf_op | source)
XLA Modules:
  0.0 2734.8 jit_solution(10114800057202767182)
XLA Ops:
  13.2 25.6 all-gather
  40.4 29.3 %all-gather.14.cloned.1.call-done = bf16[2048,1024]{1,0:T(8,128)(2,1)} async-done(((bf16[128,1024]{1,0:T(8,128)(2,1)}), bf16[2048,1024]{1,0:T(8,128)(2,1)}) %all-gather.14.cloned.1.call-update) | async-done | bytes 4194320 | tf_op jit(solution)/shard_map/all_gather | solution.py:83
  76.2 49.7 %all-gather.18.cloned.1.call-done = bf16[2048,1024]{1,0:T(8,128)(2,1)} async-done(((bf16[128,1024]{1,0:T(8,128)(2,1)}), bf16[2048,1024]{1,0:T(8,128)(2,1)}) %all-gather.18.cloned.1.call-update) | async-done | bytes 4194320 | tf_op jit(solution)/shard_map/all_gather | solution.py:84
  156.7 317.0 %all-gather.1 = bf16[16,1,128]{2,1,0:T(2,128)(2,1)S(1)} all-gather(bf16[1,1,128]{2,1,0:T(2,128)(2,1)S(1)} %convert_bitcast_fusion.2), channel_id=1, replica_groups=mesh['rep'=8,'shard'=16] {'shard'}, dimensions={0}, use_global_device_ids=true | all-gather | bytes 4352 | tf_op jit(solution)/shard_map/all_gather | solution.py:160
  504.2 73.6 %all-gather.20.cloned.1.call-done = bf16[4096,1024]{1,0:T(8,128)(2,1)} async-done(((bf16[256,1024]{1,0:T(8,128)(2,1)}), bf16[4096,1024]{1,0:T(8,128)(2,1)}) %all-gather.20.cloned.1.call-update) | async-done | bytes 8388624 | tf_op jit(solution)/shard_map/all_gather | solution.py:107
  577.8 118.2 %while.33 = (s32[]{:T(128)}, bf16[8,512,128]{2,1,0:T(8,128)(2,1)}, f32[8,512,1]{1,2,0:T(1,128)S(1)}, s32[8]{0:T(128)S(1)}, bf16[8,512,128]{2,1,0:T(8,128)(2,1)},...) while((s32[]{:T(128)}, bf16[8,512,128]{2,1,0:T(8,128)(2,1)}, ...), condition=%wide.region_6.7_spmd.clone.clone, body=%wide.region_3.6_spmd.clone.sunk.clone | while | flops 1098907136 | bytes 39211212 | solution.py:145
  722.8 77.1 %all-gather.24.cloned.1.call-done = bf16[2048,6144]{1,0:T(8,128)(2,1)} async-done(((bf16[128,6144]{1,0:T(8,128)(2,1)}), bf16[2048,6144]{1,0:T(8,128)(2,1)}) %all-gather.24.cloned.1.call-update) | async-done | bytes 25165840 | tf_op jit(solution)/shard_map/all_gather | solution.py:165
  814.2 133.9 %all-gather.26.cloned.1.call-done = bf16[2048,6144]{1,0:T(8,128)(2,1)} async-done(((bf16[128,6144]{1,0:T(8,128)(2,1)}), bf16[2048,6144]{1,0:T(8,128)(2,1)}) %all-gather.26.cloned.1.call-update) | async-done | bytes 25165840 | tf_op jit(solution)/shard_map/all_gather | solution.py:175
  948.1 20.4 multiply_convert_fusion.1
  968.5 127.2 %all-gather.28.cloned.1.call-done = bf16[2048,6144]{1,0:T(8,128)(2,1)} async-done(((bf16[128,6144]{1,0:T(8,128)(2,1)}), bf16[2048,6144]{1,0:T(8,128)(2,1)}) %all-gather.28.cloned.1.call-update) | async-done | bytes 25165840 | tf_op jit(solution)/shard_map/all_gather | solution.py:192
  1146.9 225.8 %while.34 = (s32[]{:T(128)}, f32[8,512,128]{2,1,0:T(8,128)}, bf16[4096,1024]{1,0:T(8,128)(2,1)}, bf16[4096,1024]{1,0:T(8,128)(2,1)}, bf16[8,512,128]{2,1,0:T(8,1...) while((s32[]{:T(128)}, f32[8,512,128]{2,1,0:T(8,128)}, ...), condition=%wide.region_11.12_spmd.clone.clone, body=%wide.region_9.11_spmd.clone.sunk.clone | while | flops 2703818240 | bytes 139208960 | solution.py:254
  1390.4 31.8 %copy.74 = bf16[2048,6144]{1,0:T(8,128)(2,1)} copy(bf16[2048,6144]{0,1:T(8,128)(2,1)} %convert_bitcast_fusion) | data formatting | bytes 50331648
  1450.4 20.9 reduce-scatter.12.cloned.1.call-done
  1481.7 94.9 %reduce-scatter.14.cloned.1.call-done = bf16[256,1024]{1,0:T(8,128)(2,1)} async-done(((bf16[4096,1024]{1,0:T(8,128)(2,1)}), bf16[256,1024]{1,0:T(8,128)(2,1)}) %reduce-scatter.14.cloned.1.call-update) | async-done | bytes 524304 | tf_op jit(solution)/shard_map/reduce_scatter | solution.py:259
  1582.3 19.1 convolution_convert_fusion.1
  1601.7 18.1 convolution_convert_fusion
  1619.9 150.5 %reduce-scatter.28.cloned.1.call-done = bf16[128,6144]{1,0:T(8,128)(2,1)} async-done(((bf16[2048,6144]{1,0:T(8,128)(2,1)}), bf16[128,6144]{1,0:T(8,128)(2,1)}) %reduce-scatter.28.cloned.1.call-update) | async-done | bytes 1572880
  1773.0 101.4 %reduce-scatter.16.cloned.1.call-done = bf16[128,2048]{1,0:T(8,128)(2,1)} async-done(((bf16[2048,2048]{1,0:T(8,128)(2,1)}), bf16[128,2048]{1,0:T(8,128)(2,1)}) %reduce-scatter.16.cloned.1.call-update) | async-done | bytes 524304 | tf_op jit(solution)/shard_map/reduce_scatter | solution.py:49
  1874.4 105.3 %reduce-scatter.22.cloned.1.call-done = bf16[128,2048]{1,0:T(8,128)(2,1)} async-done(((bf16[2048,2048]{1,0:T(8,128)(2,1)}), bf16[128,2048]{1,0:T(8,128)(2,1)}) %reduce-scatter.22.cloned.1.call-update) | async-done | bytes 524304 | tf_op jit(solution)/shard_map/reduce_scatter | solution.py:49
  1979.7 82.8 %reduce-scatter.18.cloned.1.call-done = bf16[128,1024]{1,0:T(8,128)(2,1)} async-done(((bf16[2048,1024]{1,0:T(8,128)(2,1)}), bf16[128,1024]{1,0:T(8,128)(2,1)}) %reduce-scatter.18.cloned.1.call-update) | async-done | bytes 262160 | tf_op jit(solution)/shard_map/reduce_scatter | solution.py:49
  2062.5 83.7 %reduce-scatter.20.cloned.1.call-done = bf16[128,1024]{1,0:T(8,128)(2,1)} async-done(((bf16[2048,1024]{1,0:T(8,128)(2,1)}), bf16[128,1024]{1,0:T(8,128)(2,1)}) %reduce-scatter.20.cloned.1.call-update) | async-done | bytes 262160 | tf_op jit(solution)/shard_map/reduce_scatter | solution.py:49
  2146.2 194.1 %reduce-scatter.24.cloned.1.call-done = bf16[128,6144]{1,0:T(8,128)(2,1)} async-done(((bf16[2048,6144]{1,0:T(8,128)(2,1)}), bf16[128,6144]{1,0:T(8,128)(2,1)}) %reduce-scatter.24.cloned.1.call-update) | async-done | bytes 1572880 | tf_op jit(solution)/shard_map/reduce_scatter | solution.py:49
  2340.3 192.3 %reduce-scatter.26.cloned.1.call-done = bf16[128,6144]{1,0:T(8,128)(2,1)} async-done(((bf16[2048,6144]{1,0:T(8,128)(2,1)}), bf16[128,6144]{1,0:T(8,128)(2,1)}) %reduce-scatter.26.cloned.1.call-update) | async-done | bytes 1572880 | tf_op jit(solution)/shard_map/reduce_scatter | solution.py:49
  2561.7 148.8 %all-reduce.4 = (f32[2048]{0:T(1024)S(1)}, f32[128]{0:T(128)}, f32[128]{0:T(128)}, f32[2048]{0:T(1024)S(1)}) all-reduce(f32[2048]{0:T(1024)S(1)} %get-tuple-element.356, f32[128]{0:T(128)S(1)} %copy-done.55, f32[128]{0:T(128)S(1)} %get-tuple-element.358, f32[2048]{0:T(1024)S(1)} %copy-done.50), channel_id=1, replica_groups=mesh['rep'=8,'shard'=16] {'rep','shard'}, use_global_device_ids=true, to_apply=%region_18.19 | all-reduce | flops 4352 | bytes 34816 | tf_op jit(solution)/shard_map/psum | solution.py:293
  (397 shorter events, 600.6 us)
Async XLA Ops:
  7.2 62.6 %all-gather.14.cloned.1.call-start = ((), (), s32[]{:S(2)}) async-start(), calls=%async_computation.11 | async-start | bytes 4456448 | tf_op jit(solution)/shard_map/all_gather | solution.py:83
  9.1 116.8 %all-gather.18.cloned.1.call-start = ((), (), s32[]{:S(2)}) async-start(), calls=%async_computation.13 | async-start | bytes 4456448 | tf_op jit(solution)/shard_map/all_gather | solution.py:84
  11.0 465.1 %all-gather.12.cloned.1.call-start = ((), (), s32[]{:S(2)}) async-start(), calls=%async_computation.10 | async-start | bytes 8912896 | tf_op jit(solution)/shard_map/all_gather | solution.py:82
  13.2 491.0 %all-gather.16.cloned.1.call-start = ((), (), s32[]{:S(2)}) async-start(), calls=%async_computation.12 | async-start | bytes 8912896 | tf_op jit(solution)/shard_map/all_gather | solution.py:106
  38.9 437.2 %copy-start.36 = (f32[16,1,128]{2,1,0:T(1,128)}, f32[16,1,128]{2,1,0:T(1,128)S(1)}, u32[]{:S(2)}) copy-start(f32[16,1,128]{2,1,0:T(1,128)S(1)} %convert_element_type.240) | copy-start | bytes 24580
  39.9 436.2 %copy-start.42 = (f32[256]{0:T(256)}, f32[256]{0:T(256)S(1)}, u32[]{:S(2)}) copy-start(f32[256]{0:T(256)S(1)} %fusion.64) | copy-start | bytes 3076
  40.4 446.2 %copy-start.23 = (f32[256,64]{1,0:T(8,128)}, f32[256,64]{1,0:T(8,128)S(1)}, u32[]{:S(2)}) copy-start(f32[256,64]{1,0:T(8,128)S(1)} %get-tuple-element.424) | copy-start | bytes 196612
  40.4 446.2 %copy-start.25 = (f32[256,64]{1,0:T(8,128)}, f32[256,64]{1,0:T(8,128)S(1)}, u32[]{:S(2)}) copy-start(f32[256,64]{1,0:T(8,128)S(1)} %get-tuple-element.425) | copy-start | bytes 196612
  76.2 501.6 %all-gather.20.cloned.1.call-start = ((), (), s32[]{:S(2)}) async-start(), calls=%async_computation.14 | async-start | bytes 8912896 | tf_op jit(solution)/shard_map/all_gather | solution.py:107
  130.2 568.1 %all-gather.22.cloned.1.call-start = ((), (), s32[]{:S(2)}) async-start(), calls=%async_computation.15 | async-start | bytes 8912896 | tf_op jit(solution)/shard_map/all_gather | solution.py:85
  131.2 668.7 %all-gather.24.cloned.1.call-start = ((), (), s32[]{:S(2)}) async-start(), calls=%async_computation.16 | async-start | bytes 26738688 | tf_op jit(solution)/shard_map/all_gather | solution.py:165
  134.5 813.6 %all-gather.26.cloned.1.call-start = ((), (), s32[]{:S(2)}) async-start(), calls=%async_computation.17 | async-start | bytes 26738688 | tf_op jit(solution)/shard_map/all_gather | solution.py:175
  137.9 957.9 %all-gather.28.cloned.1.call-start = ((), (), s32[]{:S(2)}) async-start(), calls=%async_computation.18 | async-start | bytes 26738688 | tf_op jit(solution)/shard_map/all_gather | solution.py:192
  151.0 555.3 %all-to-all-start = ((bf16[16,128,6144]{2,1,0:T(8,128)(2,1)}), bf16[16,128,6144]{2,1,0:T(8,128)(2,1)}, u32[]{:S(2)}, u32[]{:S(2)}) async-start(bf16[16,128,6144]{2,1,0:T(8,128)(2,1)} %stack.2), calls=%async_computation | async-start | bytes 50331648 | tf_op jit(solution)/shard_map/all_to_all | solution.py:162
  156.6 1314.7 %reduce-scatter.12.cloned.1.call-start = ((), (), s32[]{:S(2)}) async-start(), calls=%async_computation.19 | async-start | bytes 8912896 | tf_op jit(solution)/shard_map/reduce_scatter | solution.py:256
  1372.6 204.0 %reduce-scatter.14.cloned.1.call-start = ((), (), s32[]{:S(2)}) async-start(), calls=%async_computation.20 | async-start | bytes 8912896 | tf_op jit(solution)/shard_map/reduce_scatter | solution.py:259
  1373.4 397.0 %reduce-scatter.28.cloned.1.call-start = ((), (), s32[]{:S(2)}) async-start(), calls=%async_computation.27 | async-start | bytes 26738688
  1422.2 452.1 %reduce-scatter.16.cloned.1.call-start = ((), (), s32[]{:S(2)}) async-start(), calls=%async_computation.21 | async-start | bytes 8912896 | tf_op jit(solution)/shard_map/reduce_scatter | solution.py:49
  1441.8 537.8 %reduce-scatter.22.cloned.1.call-start = ((), (), s32[]{:S(2)}) async-start(), calls=%async_computation.24 | async-start | bytes 8912896 | tf_op jit(solution)/shard_map/reduce_scatter | solution.py:49
  1450.3 612.1 %reduce-scatter.18.cloned.1.call-start = ((), (), s32[]{:S(2)}) async-start(), calls=%async_computation.22 | async-start | bytes 4456448 | tf_op jit(solution)/shard_map/reduce_scatter | solution.py:49
  1481.7 664.5 %reduce-scatter.20.cloned.1.call-start = ((), (), s32[]{:S(2)}) async-start(), calls=%async_computation.23 | async-start | bytes 4456448 | tf_op jit(solution)/shard_map/reduce_scatter | solution.py:49
  1581.1 759.2 %reduce-scatter.24.cloned.1.call-start = ((), (), s32[]{:S(2)}) async-start(), calls=%async_computation.25 | async-start | bytes 26738688 | tf_op jit(solution)/shard_map/reduce_scatter | solution.py:49
  1601.5 931.2 %reduce-scatter.26.cloned.1.call-start = ((), (), s32[]{:S(2)}) async-start(), calls=%async_computation.26 | async-start | bytes 26738688 | tf_op jit(solution)/shard_map/reduce_scatter | solution.py:49
  1619.9 1095.0 %all-reduce.8.cloned.1.call-start = ((), (), s32[]{:S(2)}) async-start(), calls=%async_computation.28 | async-start | bytes 12582912 | tf_op jit(solution)/shard_map/psum | solution.py:305
  (68 other events, 785.7 us)
Sparse Core Ops, SparseCore 0:
  11.1 58.6 all-gather.13
  72.8 53.0 all-gather.17
  128.9 230.9 all-gather.11
  362.9 141.2 all-gather.15
  507.1 70.6 all-gather.19
  580.7 70.6 all-gather.21
  654.5 145.3 all-gather.23
  802.9 145.1 all-gather.25
  950.6 145.1 all-gather.27
  1372.8 98.4 reduce-scatter.11
  1475.5 101.0 reduce-scatter.13
  1580.8 189.5 reduce-scatter.27
  1774.7 99.6 reduce-scatter.15
  1878.5 101.1 reduce-scatter.21
  1983.5 78.8 reduce-scatter.17
  2066.9 79.2 reduce-scatter.19
  2150.4 189.8 reduce-scatter.23
  2344.5 188.0 reduce-scatter.25
  2536.3 146.2 all-reduce.7
